TPU v7x, 512 devices: a whole 4x8x8 slice. The times are simulated.
512 devices in a mesh: tm: 64 (over x, y, core), space: 8 (over z).
Axes of the slice: x: 4, y: 8, z: 8, core: 2. Of those that a mesh axis runs over, the one named last changes fastest.
Arguments:
- frames_feat: bfloat16 [64, 16, 64, 256], P('tm', 'space'), may hold values from -16 to 16
- prompt_labels: int32 [16, 64], P('space'), may hold values from 0 to 3
- label_table: float32 [4, 256], replicated, may hold values from -6 to 6
- enc_qkv: bfloat16 [256, 768], replicated, may hold values from -0.375 to 0.375
- enc_out: bfloat16 [256, 256], replicated, may hold values from -0.375 to 0.375
- norm_gain: float32 [256], replicated, may hold values from 0.25 to 1.75
- key_proj: bfloat16 [256, 1024], replicated, may hold values from -0.375 to 0.375
- value_proj: bfloat16 [256, 1024], replicated, may hold values from -0.375 to 0.375
- read_proj: bfloat16 [1024, 256], replicated, may hold values from -0.1875 to 0.1875
- decay: float32 [64, 8], P('tm'), may hold values from 0.1 to 1
- dec_conv: bfloat16 [3, 3, 256, 64], replicated, may hold values from -0.125 to 0.125
- dec_up: bfloat16 [64, 16], replicated, may hold values from -0.75 to 0.75
Outputs:
- mask_logits: float32 [64, 64, 256], P('tm', 'space')
All inputs are finite; a program needn't handle non-finite values.
Results may differ from a plain program's by a relative error of at most 0.011.
The roundings to bfloat16 on the way count: a program that leaves them out, or rounds other values in their place, can miss the bound.
Values may be sent and summed in bfloat16 or wider, within the bound.
A program may use at most 64 MiB of HBM per device.

v0:
```python
import jax
import jax.numpy as jnp
from jax import lax
from jax.sharding import Mesh
from jax.sharding import PartitionSpec as P

ENC_HEADS = 8
UP = 4
TM = ("tm_0", "tm_1", "tm_2")


epsilon = 1e-06
lowest = -1e30
precise_result = lax.Precision.HIGHEST


def laid_out(blocks, dim):
    shape = list(blocks.shape[1:])
    shape[dim] *= blocks.shape[0]
    return jnp.moveaxis(blocks, 0, dim).reshape(shape)


def from_everyone(x, axis):
    devices = lax.axis_size(axis)
    return lax.all_to_all(jnp.broadcast_to(x[None], (devices, *x.shape)), axis, 0, 0, tiled=True)


def collect(x, axis, dim):
    return laid_out(from_everyone(x, axis), dim)


def in_blocks(x, dim, devices):
    before, after = (x.shape[:dim], x.shape[dim + 1 :])
    return jnp.moveaxis(x.reshape(*before, devices, -1, *after), dim, 0)


def summed_on_arrival(x, axis, dim):
    devices = lax.axis_size(axis)
    blocks = lax.all_to_all(in_blocks(x, dim, devices), axis, 0, 0, tiled=True)
    return jnp.sum(blocks, axis=0)


def nothing_yet(x, identity):
    return jax.tree.map(
        lambda part, zero: jnp.zeros_like(part) + jnp.asarray(zero, part.dtype), x, identity
    )


def all_in_one(x, axis):
    leaves = jax.tree.leaves(x)
    turns = sorted(range(len(leaves)), key=lambda k: -leaves[k].size)
    width = (1, *leaves[turns[0]].shape)[-1]
    lines = [
        jnp.pad(leaves[k].reshape(-1), (0, -leaves[k].size % width)).reshape(-1, width)
        for k in turns
    ]
    both, at, found = (lax.all_gather(jnp.concatenate(lines), axis), 0, {})
    for k, line in zip(turns, lines):
        slab = both[:, at : at + len(line)].reshape(len(both), -1)
        found[k] = slab[:, : leaves[k].size].reshape(-1, *leaves[k].shape)
        at += len(line)
    numbers = iter(range(len(leaves)))
    return jax.tree.map(lambda _: found[next(numbers)], x)


def carried_in(x, axes, combine, identity):
    before = start = nothing_yet(x, identity)
    so_far = x
    for axis in reversed(axes):
        devices, place = (lax.axis_size(axis), lax.axis_index(axis))
        pieces = all_in_one(so_far, axis)
        inside, so_far = (start, start)
        for k in range(devices):
            passed = k < place
            so_far = combine(so_far, jax.tree.map(lambda part: part[k], pieces))
            inside = jax.tree.map(lambda new, old: jnp.where(passed, new, old), so_far, inside)
        before = combine(inside, before)
    return before


def extended(cells, sides, width):
    for axis, dim in sides:
        count = lax.axis_size(axis)
        ends = count - 1
        head = lax.slice_in_dim(cells, 0, width, axis=dim)
        tail = lax.slice_in_dim(cells, cells.shape[dim] - width, cells.shape[dim], axis=dim)
        cells = jnp.concatenate(
            [
                lax.ppermute(tail, axis, [(i, (i + 1) % count) for i in range(ends)]),
                cells,
                lax.ppermute(head, axis, [((i + 1) % count, i) for i in range(ends)]),
            ],
            axis=dim,
        )
    return cells


def pool_pairs(features):
    frame_count, height, breadth, channels = features.shape
    grouped = features.astype(jnp.float32).reshape(
        frame_count, height // 2, 2, breadth // 2, 2, channels
    )
    return jnp.mean(grouped, axis=(2, 4)).astype(jnp.bfloat16)


def gain_norm(hidden, gain_row):
    return (
        hidden * lax.rsqrt(jnp.mean(hidden * hidden, axis=-1, keepdims=True) + epsilon) * gain_row
    )


def attend_block(carried, key_part, value_part, query_heads, head_size):
    peak, totals, summed = carried
    frame_count = key_part.shape[0]
    key_head_rows = key_part.reshape(frame_count, -1, ENC_HEADS, head_size)
    value_head_rows = value_part.reshape(frame_count, -1, ENC_HEADS, head_size)
    scores = jnp.einsum(
        "ftha,fnha->fhtn", query_heads, key_head_rows, preferred_element_type=jnp.float32
    ) * head_size ** (-0.5)
    newest = jnp.maximum(peak, jnp.max(scores, axis=-1))
    weights = jnp.exp(scores - newest[..., None])
    totals = jnp.sum(weights, axis=-1)
    summed = jnp.einsum(
        "fhtn,fnha->fhta",
        weights.astype(jnp.bfloat16),
        value_head_rows,
        preferred_element_type=jnp.float32,
    )
    return (newest, totals, summed)


def link(earlier, later):
    return (earlier[0] * later[0], later[0][:, None, None] * earlier[1] + later[1])


def local_chain(rate_rows, states):
    product = jnp.ones(rate_rows.shape[1:], jnp.float32)
    summed = jnp.zeros(states.shape[1:], jnp.float32)
    product = product * rate_rows[0]
    summed = rate_rows[0][:, None, None] * summed + states[0]
    return (product, summed)


def spread_chain(rate_rows, incoming):
    memory = rate_rows[0][:, None, None] * incoming
    memories = [memory]
    return jnp.stack(memories, axis=0)


def shards(
    frames_feat,
    prompt_labels,
    label_table,
    enc_qkv,
    enc_out,
    norm_gain,
    key_proj,
    value_proj,
    read_proj,
    decay,
    dec_conv,
    dec_up,
):
    frame_count, tile_rows, grid_width, model_dim = frames_feat.shape
    tile_tok = tile_rows * grid_width
    frame_tokens = tile_tok * lax.axis_size("space")
    head_size = model_dim // ENC_HEADS
    flat_rows = frames_feat.reshape(frame_count, tile_tok, model_dim)
    pooled = pool_pairs(frames_feat).reshape(frame_count, tile_tok // 4, model_dim)
    queries = jnp.dot(flat_rows, enc_qkv[:, :model_dim], preferred_element_type=jnp.float32).astype(
        jnp.bfloat16
    )
    query_heads = queries.reshape(frame_count, tile_tok, ENC_HEADS, head_size)
    initial = (
        jnp.full((frame_count, ENC_HEADS, tile_tok), lowest, jnp.float32),
        jnp.zeros((frame_count, ENC_HEADS, tile_tok), jnp.float32),
        jnp.zeros((frame_count, ENC_HEADS, tile_tok, head_size), jnp.float32),
    )
    piece_kv = jnp.dot(
        collect(pooled, "space", 1), enc_qkv[:, model_dim:], preferred_element_type=jnp.float32
    ).astype(jnp.bfloat16)
    peak, totals, summed = attend_block(
        initial, piece_kv[..., :model_dim], piece_kv[..., model_dim:], query_heads, head_size
    )
    attended = (
        (summed / totals[..., None])
        .transpose(0, 2, 1, 3)
        .reshape(frame_count, tile_tok, model_dim)
        .astype(jnp.bfloat16)
    )
    hidden = flat_rows.astype(jnp.float32) + jnp.dot(
        attended, enc_out, preferred_element_type=jnp.float32
    )
    encoded = gain_norm(hidden, norm_gain).astype(jnp.bfloat16)
    key_rows = jnp.dot(encoded, key_proj, preferred_element_type=jnp.float32).astype(jnp.bfloat16)
    global_frame = lax.axis_index(TM) * frame_count + jnp.arange(frame_count)
    first_flag = (global_frame == 0).astype(jnp.float32)[:, None, None]
    one_hot = (
        prompt_labels.reshape(tile_tok, 1) == jnp.arange(label_table.shape[0])[None, :]
    ).astype(jnp.float32)
    label_rows = jnp.dot(one_hot, label_table, precision=precise_result)
    memory_in = (encoded.astype(jnp.float32) + first_flag * label_rows[None]).astype(jnp.bfloat16)
    value_rows = jnp.dot(memory_in, value_proj, preferred_element_type=jnp.float32).astype(
        jnp.bfloat16
    )
    head_count = decay.shape[1]
    key_head_rows = key_rows.reshape(frame_count, tile_tok, head_count, -1)
    value_head_rows = value_rows.reshape(frame_count, tile_tok, head_count, -1)
    partial_value = jnp.einsum(
        "fthk,fthv->fhkv", key_head_rows, value_head_rows, preferred_element_type=jnp.float32
    ) * frame_tokens ** (-0.5)
    share = head_count // lax.axis_size("space")
    states = summed_on_arrival(partial_value, "space", 1)
    rate_rows = lax.dynamic_slice_in_dim(decay, lax.axis_index("space") * share, share, 1)
    product, local_sum = local_chain(rate_rows, states)
    identity = (jnp.ones(product.shape, jnp.float32), jnp.zeros(local_sum.shape, jnp.float32))
    earlier = carried_in((product, local_sum), TM, link, identity)
    own_memory = spread_chain(rate_rows, earlier[1]).astype(jnp.bfloat16)
    memory = collect(own_memory, "space", 1)
    memory_output = jnp.einsum(
        "fthk,fhkv->fthv", key_head_rows, memory, preferred_element_type=jnp.float32
    ) * key_head_rows.shape[-1] ** (-0.5)
    memory_output = memory_output.reshape(frame_count, tile_tok, -1).astype(jnp.bfloat16)
    joined_rows = encoded.astype(jnp.float32) + jnp.dot(
        memory_output, read_proj, preferred_element_type=jnp.float32
    )
    decoder_in = joined_rows.astype(jnp.bfloat16).reshape(
        frame_count, tile_rows, grid_width, model_dim
    )
    padded = extended(decoder_in, (("space", 1),), 1)
    padded = jnp.pad(padded, ((0, 0), (0, 0), (1, 1), (0, 0)))
    convolved = jnp.zeros((frame_count, tile_rows, grid_width, dec_conv.shape[3]), jnp.float32)
    for row_shift in range(3):
        for col_shift in range(3):
            window = padded[
                :, row_shift : row_shift + tile_rows, col_shift : col_shift + grid_width, :
            ]
            convolved = convolved + jnp.dot(
                window, dec_conv[row_shift, col_shift], preferred_element_type=jnp.float32
            )
    mapped = jax.nn.gelu(convolved).astype(jnp.bfloat16)
    pixels = jnp.dot(mapped, dec_up, preferred_element_type=jnp.float32).reshape(
        frame_count, tile_rows, grid_width, UP, UP
    )
    return pixels.transpose(0, 1, 3, 2, 4).reshape(frame_count, tile_rows * UP, grid_width * UP)


def solution(mesh):
    finer = Mesh(
        mesh.devices.reshape(4, 8, 2, mesh.shape["space"]), ("tm_0", "tm_1", "tm_2", "space")
    )
    return jax.shard_map(
        shards,
        mesh=finer,
        in_specs=(
            P(TM, "space", None, None),
            P("space", None),
            P(),
            P(),
            P(),
            P(),
            P(),
            P(),
            P(),
            P(TM, None),
            P(),
            P(),
        ),
        out_specs=P(TM, "space", None),
        check_vma=False,
    )
```

profile of v0, /device:TPU:6, one launch (start us, length us, event | category | flops | bytes accessed | tf_op | source)
XLA Modules:
  0.0 137.2 jit_solution(15573543040766731705)
XLA Ops:
  0.0 0.9 convert_reduce_fusion
  1.1 0.7 broadcast_in_dim.6
  1.7 10.4 %all-to-all-start = ((bf16[8,1,32,256]{3,2,1,0:T(8,128)(2,1)}), bf16[8,1,32,256]{3,2,1,0:T(8,128)(2,1)S(1)}, u32[]{:S(2)}, u32[]{:S(2)}) async-start(bf16[8,1,32,256]{3,2,1,0:T(8,128)(2,1)} %broadcast_in_dim.6), calls=%async_computation | async-start | bytes 262144 | tf_op jit(solution)/shard_map/all_to_all | solution.py:25
  12.2 0.2 convolution_convert_fusion.3
  12.5 0.7 copy-done.10
  13.3 8.0 %all-to-all-done = bf16[8,1,32,256]{3,2,1,0:T(8,128)(2,1)S(1)} async-done(((bf16[8,1,32,256]{3,2,1,0:T(8,128)(2,1)}), bf16[8,1,32,256]{3,2,1,0:T(8,128)(2,1)S(1)}, u32[]{:S(2)}, u32[]{:S(2)}) %all-to-all-start) | async-done | bytes 131104 | tf_op jit(solution)/shard_map/all_to_all | solution.py:25
  21.3 0.2 fusion.2
  21.7 0.4 fusion.92
  22.2 0.4 fusion.10
  22.6 0.4 fusion.6
  23.0 0.5 copy-done.6
  23.5 0.3 multiply_reduce_fusion
  23.8 0.7 copy-done.7
  24.6 0.2 fusion.3
  24.8 0.4 copy-done.8
  25.3 0.3 fusion.8
  25.6 0.2 fusion.4
  25.9 1.1 fusion
  27.0 3.5 %all-to-all-start.1 = ((f32[8,1,1,128,128]{4,3,2,1,0:T(8,128)}), f32[8,1,1,128,128]{4,3,2,1,0:T(8,128)S(1)}, u32[]{:S(2)}, u32[]{:S(2)}) async-start(f32[8,1,1,128,128]{4,3,2,1,0:T(8,128)} %fusion), calls=%async_computation.1 | async-start | bytes 1048576 | tf_op jit(solution)/shard_map/all_to_all | solution.py:39
  30.5 0.6 copy-done.11
  31.2 0.6 constant_dynamic-slice_fusion
  32.4 0.6 pad_bitcast_fusion.2
  33.1 13.5 %all-to-all-done.1 = f32[8,1,1,128,128]{4,3,2,1,0:T(8,128)S(1)} async-done(((f32[8,1,1,128,128]{4,3,2,1,0:T(8,128)}), f32[8,1,1,128,128]{4,3,2,1,0:T(8,128)S(1)}, u32[]{:S(2)}, u32[]{:S(2)}) %all-to-all-start.1) | async-done | bytes 524320 | tf_op jit(solution)/shard_map/all_to_all | solution.py:39
  46.6 1.9 %all-gather.3 = f32[2,129,128]{2,1,0:T(8,128)S(1)} all-gather(f32[1,129,128]{2,1,0:T(8,128)S(1)} %maximum_bitcast_fusion), channel_id=2, replica_groups=mesh['tm_0'=4,'tm_1'=8,'tm_2'=2,'space'=8] {'tm_2'}, dimensions={0}, use_global_device_ids=true | all-gather | bytes 198144 | tf_op jit(solution)/shard_map/all_gather | solution.py:57
  48.5 0.6 fusion.91
  51.1 0.7 fusion.79
  51.8 27.2 %all-gather.4 = f32[8,129,128]{2,1,0:T(8,128)S(1)} all-gather(f32[1,129,128]{2,1,0:T(8,128)S(1)} %maximum_bitcast_fusion.1), channel_id=3, replica_groups=mesh['tm_0'=4,'tm_1'=8,'tm_2'=2,'space'=8] {'tm_1'}, dimensions={0}, use_global_device_ids=true | all-gather | bytes 594432 | tf_op jit(solution)/shard_map/all_gather | solution.py:57
  79.0 0.6 fusion.89
  86.6 4.3 %slice_add_fusion.4 = (f32[1,128,128]{2,1,0:T(8,128)S(1)}, f32[1,128,128]{2,1,0:T(8,128)S(1)}) fusion(f32[8,129,128]{2,1,0:T(8,128)S(1)} %all-gather.4, f32[]{:T(128)} %bitcast.45, f32[]{:T(128)} %bitcast.44, f32[]{:T(128)} %bitcast.47, f32[]{:T(128)} %bitcast.46, f32[]{:T(128)} %bitcast.51, f32[]{:T(128)} %bitcast.50, f32[]{:T(128)} %bitcast.49, f32[]{:T(128)} %bitcast.48), kind=kLoop, calls=%fused_computation.89 | loop fusion | flops 245760 | bytes 655392 | tf_op jit(solution)/shard_map/add | solution.py:133
  91.0 12.3 %all-gather.5 = f32[4,129,128]{2,1,0:T(8,128)S(1)} all-gather(f32[1,129,128]{2,1,0:T(8,128)S(1)} %maximum_bitcast_fusion.2), channel_id=4, replica_groups=mesh['tm_0'=4,'tm_1'=8,'tm_2'=2,'space'=8] {'tm_0'}, dimensions={0}, use_global_device_ids=true | all-gather | bytes 330240 | tf_op jit(solution)/shard_map/all_gather | solution.py:57
  103.3 0.6 fusion.90
  104.5 6.4 %fusion.78 = bf16[128,128]{1,0:T(8,128)(2,1)S(1)} fusion(f32[2,129,128]{2,1,0:T(8,128)S(1)} %all-gather.3, f32[]{:T(128)} %bitcast.20, pred[]{:T(512)} %gt.51, pred[]{:T(512)} %gt.50, f32[1,128,128]{2,1,0:T(8,128)S(1)} %get-tuple-element.5, f32[1,128,128]{2,1,0:T(8,128)S(1)} %get-tuple-element.6, f32[8,129,128]{2,1,0:T(8,128)S(1)} %all-gather.4, ...), kind=kLoop, calls=%fused_computation.125 | loop fusion | flops 671744 | bytes 950346 | tf_op jit(solution)/shard_map/convert_element_type | solution.py:218
  111.1 12.5 %all_to_all.15 = bf16[8,1,1,128,128]{3,4,2,1,0:T(8,128)(2,1)S(1)} all-to-all(bf16[8,1,1,128,128]{3,4,2,1,0:T(8,128)(2,1)S(1)} %broadcast_in_dim.8), channel_id=1, replica_groups=mesh['tm_0'=4,'tm_1'=8,'tm_2'=2,'space'=8] {'space'}, dimensions={0} | all-to-all | bytes 524288 | tf_op jit(solution)/shard_map/all_to_all | solution.py:25
  123.7 0.3 fusion.1
  124.0 0.7 copy-done.2
  124.7 0.3 fusion.7
  125.0 3.3 %collective-permute-start = (bf16[1,1,64,256]{3,2,1,0:T(8,128)(2,1)S(1)}, bf16[1,1,64,256]{3,2,1,0:T(8,128)(2,1)S(1)}, u32[]{:S(2)}, u32[]{:S(2)}) collective-permute-start(bf16[1,1,64,256]{3,2,1,0:T(8,128)(2,1)S(1)} %get-tuple-element.9), channel_id=1, source_target_pairs={{0,1},{1,2},{2,3},{3,4},{4,5},{5,6},{6,7},{8,9},{9,10},{10,11},{11... | collective-permute-start | bytes 98312 | tf_op jit(solution)/shard_map/ppermute | solution.py:89
  128.3 1.3 collective-permute-start.1
  129.6 0.3 collective-permute-done
  129.9 4.2 %collective-permute-done.1 = bf16[1,1,64,256]{3,2,1,0:T(8,128)(2,1)S(1)} collective-permute-done((bf16[1,1,64,256]{3,2,1,0:T(8,128)(2,1)S(1)}, bf16[1,1,64,256]{3,2,1,0:T(8,128)(2,1)S(1)}, u32[]{:S(2)}, u32[]{:S(2)}) %collective-permute-start.1) | collective-permute-done | bytes 32800 | tf_op jit(solution)/shard_map/ppermute | solution.py:91
  134.3 0.2 fusion.38
  134.4 0.2 convolution_add_fusion.8
  134.6 0.1 convolution_add_fusion.7
  135.1 0.1 convolution_add_fusion.4
  135.4 0.5 copy-done.9
  135.9 0.3 convolution_bitcast_fusion
  136.2 0.2 copy.76
  136.4 0.8 reshape.450
  (46 shorter events, 1.6 us)
Async XLA Ops:
  0.0 24.6 %copy-start = (bf16[256,1024]{1,0:T(8,128)(2,1)S(1)}, bf16[256,1024]{1,0:T(8,128)(2,1)}, u32[]{:S(2)}) copy-start(bf16[256,1024]{1,0:T(8,128)(2,1)} %param.18) | copy-start | bytes 1572868
  0.0 12.2 %copy-start.4 = (bf16[256,768]{1,0:T(8,128)(2,1)S(1)}, bf16[256,768]{1,0:T(8,128)(2,1)}, u32[]{:S(2)}) copy-start(bf16[256,768]{1,0:T(8,128)(2,1)} %param.15) | copy-start | bytes 1179652
  1.7 10.5 %copy-start.1 = (bf16[1,2,64,256]{3,2,1,0:T(8,128)(2,1)S(1)}, bf16[1,2,64,256]{3,2,1,0:T(8,128)(2,1)}, u32[]{:S(2)}) copy-start(bf16[1,2,64,256]{3,2,1,0:T(8,128)(2,1)} %param.12) | copy-start | bytes 196612
  1.7 19.5 %all-to-all-start = ((bf16[8,1,32,256]{3,2,1,0:T(8,128)(2,1)}), bf16[8,1,32,256]{3,2,1,0:T(8,128)(2,1)S(1)}, u32[]{:S(2)}, u32[]{:S(2)}) async-start(bf16[8,1,32,256]{3,2,1,0:T(8,128)(2,1)} %broadcast_in_dim.6), calls=%async_computation | async-start | bytes 262144 | tf_op jit(solution)/shard_map/all_to_all | solution.py:25
  12.5 0.7 copy-start.10
  22.6 0.9 copy-start.6
  23.8 0.7 copy-start.7
  24.6 0.7 copy-start.8
  24.6 1.0 copy-start.3
  27.0 19.6 %all-to-all-start.1 = ((f32[8,1,1,128,128]{4,3,2,1,0:T(8,128)}), f32[8,1,1,128,128]{4,3,2,1,0:T(8,128)S(1)}, u32[]{:S(2)}, u32[]{:S(2)}) async-start(f32[8,1,1,128,128]{4,3,2,1,0:T(8,128)} %fusion), calls=%async_computation.1 | async-start | bytes 1048576 | tf_op jit(solution)/shard_map/all_to_all | solution.py:39
  30.5 0.7 copy-start.11
  123.7 1.0 copy-start.2
  125.0 9.2 %copy-start.5 = (bf16[3,3,256,64]{2,3,1,0:T(8,128)(2,1)S(1)}, bf16[3,3,256,64]{2,3,1,0:T(8,128)(2,1)}, u32[]{:S(2)}) copy-start(bf16[3,3,256,64]{2,3,1,0:T(8,128)(2,1)} %param.22) | copy-start | bytes 884740
  125.0 4.8 %collective-permute-start = (bf16[1,1,64,256]{3,2,1,0:T(8,128)(2,1)S(1)}, bf16[1,1,64,256]{3,2,1,0:T(8,128)(2,1)S(1)}, u32[]{:S(2)}, u32[]{:S(2)}) collective-permute-start(bf16[1,1,64,256]{3,2,1,0:T(8,128)(2,1)S(1)} %get-tuple-element.9), channel_id=1, source_target_pairs={{0,1},{1,2},{2,3},{3,4},{4,5},{5,6},{6,7},{8,9},{9,10},{10,11},{11... | collective-permute-start | bytes 98312 | tf_op jit(solution)/shard_map/ppermute | solution.py:89
  128.3 5.8 %collective-permute-start.1 = (bf16[1,1,64,256]{3,2,1,0:T(8,128)(2,1)S(1)}, bf16[1,1,64,256]{3,2,1,0:T(8,128)(2,1)S(1)}, u32[]{:S(2)}, u32[]{:S(2)}) collective-permute-start(bf16[1,1,64,256]{3,2,1,0:T(8,128)(2,1)S(1)} %get-tuple-element.10), channel_id=1, source_target_pairs={{1,0},{2,1},{3,2},{4,3},{5,4},{6,5},{7,6},{9,8},{10,9},{11,10},{12... | collective-permute-start | bytes 98312 | tf_op jit(solution)/shard_map/ppermute | solution.py:91
  135.2 0.7 copy-start.9
where the time goes:
time: 138 us; the launch traced here: 137 us
  blocking collectives  53.9 us (39%)
  waiting for transfers between devices  26 us (19%)
  starting transfers between devices  18.5 us (13%)
  other arithmetic  13.1 us (9%)
  between operations  10.7 us (8%)
  local copies, waits for them, and re-layouts  9.65 us (7%)
  matrix products  5.29 us (4%)
    all_gather x3, blocking collectives, all_in_one(): both, at, found = (lax.all_gather(jnp.concatenate(lines), axis), 0, {})  41.4 us
    all_to_all x1, waiting for transfers between devices, summed_on_arrival(): blocks = lax.all_to_all(in_blocks(x, dim, devices), axis, 0, 0, tiled=True)  13.5 us
    all_to_all x1, blocking collectives, from_everyone(): lax.all_to_all(jnp.broadcast_to(x[None], (devices, *x.shape)), axis, 0, 0...  12.5 us
    all_to_all x1, starting transfers between devices, from_everyone(): lax.all_to_all(jnp.broadcast_to(x[None], (devices, *x.shape)), axis, 0, 0...  10.4 us
    all_to_all x1, waiting for transfers between devices, from_everyone(): lax.all_to_all(jnp.broadcast_to(x[None], (devices, *x.shape)), axis, 0, 0...  8.02 us
    convert_element_type x1, other arithmetic, shards(): own_memory = spread_chain(rate_rows, earlier[1]).astype(jnp.bfloat16)  6.44 us
    unnamed x24, local copies, waits for them, and re-layouts  4.38 us
    add x1, other arithmetic, link(): later[0][:, None, None] * earlier[1] + later[1]  4.35 us
  transfers between devices with their start and end apart: 4, of which 4 were waited for; matrix products, arithmetic and copies ran while one was open for 1% of the time, Pallas kernels for 0%

commit v1 on v0

v1 whole, which is shorter than its diff:
```python
import math

import jax
import jax.numpy as jnp
from jax import lax
from jax.experimental import pallas as pl
from jax.experimental.pallas import tpu as pltpu
from jax.sharding import PartitionSpec as P

MESH = pl.DeviceIdType.MESH
BF16 = jnp.bfloat16
F32 = jnp.float32

FRAMES = 64
BANDS = 8
OWNERS = 16
STRIDE = FRAMES // OWNERS
TOK = 128
DIM = 256
HEADS = 8
HEAD = DIM // HEADS
FEAT = 128
CH = 64
TAPS = 9
FAR_FIRST = (4, 3, 5, 2, 6, 1, 7)


def mm(a, b):
    return jnp.dot(a, b, preferred_element_type=F32)


def mm_nt(a, b):
    return lax.dot_general(a, b, (((1,), (1,)), ((), ())), preferred_element_type=F32)


def turned(x):
    return x.astype(F32).T.astype(x.dtype)


def iota(shape, dim):
    return lax.broadcasted_iota(jnp.int32, shape, dim)


def three_parts(x):
    high = x.astype(BF16)
    rest = x - high.astype(F32)
    middle = rest.astype(BF16)
    low = (rest - middle.astype(F32)).astype(BF16)
    return high, middle, low


def kernel(
    frames, labels, table, qkv, eo, gain, kp, vp, rp, decay, conv, up,
    out,
    x_v, lab_v, tab_v, qkv_v, eo_v, gain_v, kp_v, vp_v, rp_v, dec_v, conv_v, up_v,
    wq_t, eo_t, kp_t, vp_t, tab_t, gain_b, taps_t, up_x, spread,
    pool, hot, xt, kmask, v_t, e_t, e_tmp, k_t,
    state, states, decays, decay_own, memories, memory,
    conved, part, parts,
    load, send, pool_in, hot_in, xt_in, decay_in, state_in, memory_in, part_in,
):
    tm, sp = lax.axis_index("tm"), lax.axis_index("space")
    is_owner = lax.rem(tm, STRIDE) == 0

    barrier = pltpu.get_barrier_semaphore()
    for k in range(1, BANDS):
        pl.semaphore_signal(
            barrier, inc=1, device_id=(tm, lax.rem(sp + k, BANDS)), device_id_type=MESH
        )

    @pl.when(is_owner)
    def _():
        @pl.loop(1, FRAMES)
        def _(k):
            pl.semaphore_signal(
                barrier, inc=1, device_id=(lax.rem(tm + k, FRAMES), sp), device_id_type=MESH
            )

    @pl.when(jnp.logical_not(is_owner))
    def _():
        @pl.loop(0, OWNERS)
        def _(k):
            pl.semaphore_signal(barrier, inc=1, device_id=(k * STRIDE, sp), device_id_type=MESH)

    col = pl.multiple_of(sp * FEAT, FEAT)
    loads = [
        (frames.at[0], x_v),
        (labels, lab_v),
        (decay, dec_v),
        (qkv, qkv_v),
        (table, tab_v),
        (eo, eo_v),
        (gain, gain_v),
        (kp.at[:, pl.ds(col, FEAT)], kp_v),
        (vp.at[:, pl.ds(col, FEAT)], vp_v),
        (rp.at[pl.ds(col, FEAT), :], rp_v),
        (conv, conv_v),
        (up, up_v),
    ]
    loads = [pltpu.make_async_copy(s, d, load.at[n]) for n, (s, d) in enumerate(loads)]
    for c in loads:
        c.start()

    loads[0].wait()
    x = x_v[...].reshape(TOK, DIM)
    pr, pc = iota((TOK // 4, TOK), 0), iota((TOK // 4, TOK), 1)
    quarter = jnp.where(lax.rem(pc, 64) // 2 == pr, 0.25, 0.0).astype(BF16)
    pool[sp] = mm(quarter, x).astype(BF16)
    loads[1].wait()
    lab = lab_v[...]
    lab_row = jnp.concatenate([lab[0:1], lab[1:2]], axis=1)
    hit = (jnp.broadcast_to(lab_row, (16, TOK)) == iota((16, TOK), 0)) & (tm == 0)
    hot[sp] = jnp.where(hit, 1.0, 0.0).astype(BF16)
    loads[2].wait()
    rate = jnp.sum(
        jnp.where(iota((1, HEADS), 1) == sp, dec_v[...], 0.0), axis=1, keepdims=True
    )
    decay_own[...] = jnp.broadcast_to(rate, (8, FEAT))

    @pl.when(is_owner)
    def _():
        pl.semaphore_wait(barrier, BANDS - 1 + FRAMES - 1)

    @pl.when(jnp.logical_not(is_owner))
    def _():
        pl.semaphore_wait(barrier, BANDS - 1 + OWNERS)

    def to_band(k, buf, n, sem):
        pltpu.make_async_remote_copy(
            src_ref=buf.at[sp],
            dst_ref=buf.at[sp],
            send_sem=send.at[n],
            recv_sem=sem,
            device_id=(tm, lax.rem(sp + k, BANDS)),
            device_id_type=MESH,
        ).start()

    def arrived(ref, sem):
        pltpu.make_async_copy(ref, ref, sem).wait()

    for k in FAR_FIRST:
        to_band(k, pool, 0, pool_in)
    xt[sp] = x.astype(F32).T.astype(BF16)
    for k in (1, 7, 2, 6, 3, 5, 4):
        to_band(k, hot, 1, hot_in)
        to_band(k, xt, 2, xt_in.at[k])

    def to_owners(src, dst, n, sem):
        for c in range(OWNERS):
            @pl.when(tm != c * STRIDE)
            def _():
                pltpu.make_async_remote_copy(
                    src_ref=src(c),
                    dst_ref=dst.at[tm],
                    send_sem=send.at[n],
                    recv_sem=sem,
                    device_id=(c * STRIDE, sp),
                    device_id_type=MESH,
                ).start()

    to_owners(lambda c: decay_own, decays, 3, decay_in)

    for c in loads[3:]:
        c.wait()
    wq_t[...] = turned(qkv_v[:, :DIM])
    eo_t[...] = turned(eo_v[...])
    kp_t[...] = turned(kp_v[...])
    vp_t[...] = turned(vp_v[...])
    tab = jnp.concatenate([tab_v[...], jnp.zeros((12, DIM), F32)], axis=0)
    tab_t[...] = turned(jnp.concatenate(three_parts(tab), axis=0))
    gain_b[...] = jnp.broadcast_to(gain_v[...], (TOK, DIM)).T

    @pl.loop(0, TAPS)
    def _(n):
        tap = conv_v[n]
        both = mm(rp_v[...], tap).T.astype(BF16)
        own = conv_v[n, pl.ds(pl.multiple_of(sp * HEAD, HEAD), HEAD), :].astype(F32).T.astype(BF16)
        taps_t[pl.ds(pl.multiple_of(n * CH, CH), CH), :] = jnp.concatenate([both, own], axis=1)

    row, src_row = iota((32, 16), 0), iota((32, 16), 1)
    picks = jnp.where(src_row == 4 * lax.rem(row, 4) + row // 8, 1.0, 0.0).astype(BF16)
    up_x[...] = mm_nt(picks, up_v[...]).astype(BF16)
    er, ec = iota((4 * TOK, DIM), 0), iota((4 * TOK, DIM), 1)
    spread[...] = jnp.where(ec == 4 * lax.rem(er, 64) + er // TOK, 1.0, 0.0).astype(BF16)

    arrived(pool.at[pl.ds(0, BANDS - 1)], pool_in)
    pooled = pool[...].reshape(BANDS * TOK // 4, DIM)
    kv = mm(pooled, qkv_v[:, DIM:])
    keys = kv[:, :DIM].astype(BF16)
    v_t[...] = kv[:, DIM:].T.astype(BF16)
    lane_head = iota((DIM, DIM), 1) // HEAD
    for h in range(HEADS):
        kmask[h] = jnp.where(lane_head == h, keys, jnp.zeros_like(keys))
    arrived(hot.at[pl.ds(0, BANDS - 1)], hot_in)

    state[...] = jnp.zeros_like(state)
    factor = HEAD**-0.5 * math.log2(math.e)

    @pl.loop(0, BANDS // 2)
    def _(p):
        k0, k1 = p, BANDS - 1 - p

        @pl.when(p > 0)
        def _():
            arrived(xt.at[0], xt_in.at[k0])

        arrived(xt.at[0], xt_in.at[k1])
        b0, b1 = lax.rem(sp + BANDS - k0, BANDS), lax.rem(sp + BANDS - k1, BANDS)
        xp = jnp.concatenate([xt[b0], xt[b1]], axis=1)
        q = mm(wq_t[...], xp).astype(BF16)
        attended = []
        for h in range(HEADS):
            s = mm(kmask[h], q)
            w = jnp.exp2((s - jnp.max(s, axis=0, keepdims=True)) * factor)
            total = jnp.sum(w, axis=0, keepdims=True)
            a = mm(v_t[h * HEAD : (h + 1) * HEAD, :], w.astype(BF16))
            attended.append((a / total).astype(BF16))
        hidden = xp.astype(F32) + mm(eo_t[...], jnp.concatenate(attended, axis=0))
        scale = lax.rsqrt(jnp.mean(hidden * hidden, axis=0, keepdims=True) + 1e-06)
        gains = jnp.concatenate([gain_b[...], gain_b[...]], axis=1)
        encoded = (hidden * scale * gains).astype(BF16)
        e_tmp[...] = encoded
        own = e_tmp[pl.ds(pl.multiple_of(sp * HEAD, HEAD), HEAD), :]
        e_t[b0] = own[:, :TOK]
        e_t[b1] = own[:, TOK:]
        key = mm(kp_t[...], encoded).astype(BF16)
        k_t[b0] = key[:, :TOK]
        k_t[b1] = key[:, TOK:]
        mark = jnp.concatenate([hot[b0], hot[b1]], axis=1)
        mark = jnp.concatenate([mark, mark, mark], axis=0)
        told = (encoded.astype(F32) + mm(tab_t[...], mark)).astype(BF16)
        value = mm(vp_t[...], told).astype(BF16)
        state[...] += mm_nt(value, key).reshape(OWNERS, 8, FEAT)

    state[...] = state[...] * (BANDS * TOK) ** -0.5

    to_owners(lambda c: state.at[c], states, 4, state_in)

    @pl.when(is_owner)
    def _():
        states[tm] = state[tm // STRIDE]
        decays[tm] = decay_own[...]
        arrived(decays.at[pl.ds(0, FRAMES - 1)], decay_in)
        arrived(states.at[pl.ds(0, FRAMES - 1)], state_in)
        place = tm // STRIDE

        def frame(t, held):
            held = decays[t] * held
            memories[t] = held

            @pl.when(t != tm)
            def _():
                pltpu.make_async_remote_copy(
                    src_ref=memories.at[t],
                    dst_ref=memory.at[place],
                    send_sem=send.at[5],
                    recv_sem=memory_in,
                    device_id=(t, sp),
                    device_id_type=MESH,
                ).start()

            return held + states[t]

        lax.fori_loop(0, FRAMES, frame, jnp.zeros((8, FEAT), F32))
        memory[place] = memories[tm]
        arrived(memory.at[pl.ds(0, OWNERS - 1)], memory_in)

    @pl.when(jnp.logical_not(is_owner))
    def _():
        arrived(memory, memory_in)

    now = memory[...].reshape(FEAT, FEAT).astype(BF16)
    for p in range(BANDS // 2):
        key = jnp.concatenate([k_t[2 * p], k_t[2 * p + 1]], axis=1)
        own = jnp.concatenate([e_t[2 * p], e_t[2 * p + 1]], axis=1)
        read = (mm(now, key) * FEAT**-0.5).astype(BF16)
        c = mm(taps_t[...], jnp.concatenate([read, own], axis=0))
        conved[2 * p] = c[:, :TOK]
        conved[2 * p + 1] = c[:, TOK:]
    lane = iota((CH, TOK), 1)
    column = lax.rem(lane, 64)

    def tap(n, a, b):
        at = (a * 3 + b) * CH
        return conved[n, at : at + CH, :]

    for n in range(BANDS):
        shifted = []
        for b in range(3):
            late, early = tap(n, 2, b), tap(n, 0, b)
            if n > 0:
                late = late + tap(n - 1, 0, b)
            if n < BANDS - 1:
                early = early + tap(n + 1, 2, b)
            shifted.append(tap(n, 1, b) + pltpu.roll(jnp.where(lane >= 64, late, early), 64, 1))
        total = shifted[1]
        total = total + jnp.where(column != 63, pltpu.roll(shifted[2], TOK - 1, 1), 0.0)
        total = total + jnp.where(column != 0, pltpu.roll(shifted[0], 1, 1), 0.0)
        part[n] = total.astype(BF16)

        @pl.when(sp != n)
        def _():
            pltpu.make_async_remote_copy(
                src_ref=part.at[n],
                dst_ref=parts.at[sp],
                send_sem=send.at[6],
                recv_sem=part_in,
                device_id=(tm, n),
                device_id_type=MESH,
            ).start()

    parts[sp] = part[sp]
    arrived(parts.at[pl.ds(0, BANDS - 1)], part_in)
    total = parts[0].astype(F32)
    for n in range(1, BANDS):
        total = total + parts[n].astype(F32)
    cubic = total + 0.044715 * (total * total * total)
    hidden = (0.5 * total * (1.0 + jnp.tanh(math.sqrt(2 / math.pi) * cubic))).astype(BF16)
    pixels = mm(up_x[...], hidden)
    keep = (lax.rem(iota((32, TOK), 0) // 4, 2)) == (iota((32, TOK), 1) // 64)
    pixels = jnp.where(keep, pixels, 0.0)
    wide = jnp.concatenate([pixels[8 * b : 8 * b + 8] for b in range(4)], axis=1)
    high, middle, low = three_parts(wide)
    high = mm(high, spread[...])
    out[0] = high + (mm(middle, spread[...]) + mm(low, spread[...]))

    arrived(pool.at[pl.ds(0, BANDS - 1)], send.at[0])
    arrived(hot.at[pl.ds(0, BANDS - 1)], send.at[1])
    arrived(xt.at[pl.ds(0, BANDS - 1)], send.at[2])

    @pl.when(is_owner)
    def _():
        arrived(state.at[pl.ds(0, OWNERS - 1)], send.at[3])
        arrived(state.at[pl.ds(0, OWNERS - 1)], send.at[4])
        arrived(memories.at[pl.ds(0, FRAMES - 1)], send.at[5])

    @pl.when(jnp.logical_not(is_owner))
    def _():
        arrived(state, send.at[3])
        arrived(state, send.at[4])

    arrived(part.at[pl.ds(0, BANDS - 1)], send.at[6])


def shards(frames, labels, table, qkv, eo, gain, kp, vp, rp, decay, conv, up):
    vmem = pltpu.VMEM
    dma = pltpu.SemaphoreType.DMA
    scratch = [
        vmem((2, 64, DIM), BF16), vmem((2, 64), jnp.int32), vmem((4, DIM), F32),
        vmem((DIM, 3 * DIM), BF16), vmem((DIM, DIM), BF16), vmem((1, DIM), F32),
        vmem((DIM, FEAT), BF16), vmem((DIM, FEAT), BF16), vmem((FEAT, DIM), BF16),
        vmem((1, HEADS), F32), vmem((TAPS, DIM, CH), BF16), vmem((CH, 16), BF16),
        vmem((DIM, DIM), BF16), vmem((DIM, DIM), BF16), vmem((FEAT, DIM), BF16),
        vmem((FEAT, DIM), BF16), vmem((DIM, 48), BF16), vmem((DIM, TOK), F32),
        vmem((TAPS * CH, FEAT + HEAD), BF16), vmem((32, CH), BF16), vmem((4 * TOK, DIM), BF16),
        vmem((BANDS, TOK // 4, DIM), BF16), vmem((BANDS, 16, TOK), BF16),
        vmem((BANDS, DIM, TOK), BF16), vmem((HEADS, DIM, DIM), BF16), vmem((DIM, DIM), BF16),
        vmem((BANDS, HEAD, TOK), BF16), vmem((DIM, 2 * TOK), BF16), vmem((BANDS, FEAT, TOK), BF16),
        vmem((OWNERS, 8, FEAT), F32), vmem((FRAMES, 8, FEAT), F32), vmem((FRAMES, 8, FEAT), F32),
        vmem((8, FEAT), F32), vmem((FRAMES, 8, FEAT), F32), vmem((OWNERS, 8, FEAT), F32),
        vmem((BANDS, TAPS * CH, TOK), F32), vmem((BANDS, CH, TOK), BF16),
        vmem((BANDS, CH, TOK), BF16),
        dma((12,)), dma((7,)), dma, dma, dma((BANDS,)), dma, dma, dma, dma,
    ]
    return pl.pallas_call(
        kernel,
        out_shape=jax.ShapeDtypeStruct((1, 8, DIM), F32),
        in_specs=[pl.BlockSpec(memory_space=pl.ANY)] * 12,
        out_specs=pl.BlockSpec(memory_space=pltpu.VMEM),
        scratch_shapes=scratch,
        compiler_params=pltpu.CompilerParams(
            collective_id=0, has_side_effects=True, vmem_limit_bytes=48 * 1024 * 1024
        ),
        name="propagate",
    )(
        frames, labels, table, qkv, eo, gain.reshape(1, DIM), kp, vp, rp, decay,
        conv.reshape(TAPS, DIM, CH), up,
    )


def solution(mesh):
    return jax.shard_map(
        shards,
        mesh=mesh,
        in_specs=(
            P("tm", "space", None, None), P("space", None), P(), P(), P(), P(), P(), P(), P(),
            P("tm", None), P(), P(),
        ),
        out_specs=P("tm", "space", None),
        check_vma=False,
    )
```

time: 138 us -> 69.4 us (0.50)
  Pallas kernels: 0 us -> 62.1 us
  blocking collectives: 53.9 us -> 0 us
  waiting for transfers between devices: 26 us -> 0 us
  starting transfers between devices: 18.5 us -> 0 us
  other arithmetic: 13.1 us -> 0 us
  between operations: 10.7 us -> 0.1 us
  matrix products: 5.29 us -> 0 us
  local copies, waits for them, and re-layouts: 9.65 us -> 6.48 us
    pallas_call x0 -> x1, Pallas kernels: none -> 62.1 us  [shards(): pl.pallas_call(kernel, out_shape=jax.ShapeDtypeStruct((1, 8, DIM), F32),...]
    all_gather x3 -> x0, blocking collectives: 41.4 us -> none  [all_in_one(): both, at, found = (lax.all_gather(jnp.concatenate(lines), axis), 0, {})]
    all_to_all x2 -> x0, waiting for transfers between devices: 21.5 us -> none  [the longest x1 13.5 us: summed_on_arrival(): blocks = lax.all_to_all(in_blocks(x, dim, devices), axis, 0, 0, tiled=True)]
    all_to_all x2 -> x0, starting transfers between devices: 13.9 us -> none  [the longest x1 10.4 us: from_everyone(): lax.all_to_all(jnp.broadcast_to(x[None], (devices, *x.shape)), axis, 0, 0...]
    all_to_all x1 -> x0, blocking collectives: 12.5 us -> none  [from_everyone(): lax.all_to_all(jnp.broadcast_to(x[None], (devices, *x.shape)), axis, 0, 0...]
    convert_element_type x3 -> x0, other arithmetic: 6.53 us -> none  [the longest x1 6.44 us: shards(): own_memory = spread_chain(rate_rows, earlier[1]).astype(jnp.bfloat16)]
    dot_general x20 -> x0, matrix products: 5.29 us -> none  [the longest x8 1.16 us: shards(): jnp.dot(window, dec_conv[row_shift, col_shift], preferred_element_type=jn...]
    ppermute x2 -> x0, starting transfers between devices: 4.55 us -> none  [the longest x1 3.26 us: extended(): lax.ppermute(tail, axis, [(i, (i + 1) % count) for i in range(ends)])]
  transfers between devices with their start and end apart: 4 -> 0, of which waited for: 4 -> 0; matrix products, arithmetic and copies ran while one was open for 1% -> 0% of each run, Pallas kernels for 0% -> 0%
where the time goes in v1:
time: 69.4 us; the launch traced here: 68.6 us
  Pallas kernels  62.1 us (89%)
  local copies, waits for them, and re-layouts  6.48 us (9%)
    pallas_call x1, Pallas kernels, shards(): pl.pallas_call(kernel, out_shape=jax.ShapeDtypeStruct((1, 8, DIM), F32),...  62.1 us
    unnamed x23, local copies, waits for them, and re-layouts  6.48 us

profile of v1, /device:TPU:6, one launch (start us, length us, event | category | flops | bytes accessed | tf_op | source)
XLA Modules:
  0.0 68.6 jit_solution(17681247871630159414)
XLA Ops:
  0.0 0.0 copy-start
  0.0 0.8 %copy.14.up = bf16[64,16]{1,0:T(8,128)(2,1)S(1)} copy(bf16[64,16]{0,1:T(8,128)(2,1)} %param.23) | data formatting | bytes 4096 | tf_op args[11]
  0.8 0.0 copy-start.4
  0.8 0.0 copy-start.5
  0.9 0.0 copy-start.6
  0.9 0.0 copy-start.8
  0.9 1.3 %copy.13 = bf16[3,3,256,64]{3,2,1,0:T(8,128)(2,1)S(1)} copy(bf16[3,3,256,64]{2,3,1,0:T(8,128)(2,1)} %param.22) | data formatting | bytes 589824 | tf_op args[10]
  2.2 0.0 copy-start.7
  2.2 0.0 copy-start.9
  2.2 0.0 copy-done
  2.2 0.0 copy-done.4
  2.2 0.0 copy-done.5
  2.3 0.0 copy-done.6
  2.3 0.0 copy-done.8
  2.3 0.6 copy-done.7
  2.9 0.0 copy-done.9
  2.9 0.0 copy-start.1
  2.9 1.0 %copy-done.1 = bf16[256,1024]{1,0:T(8,128)(2,1)S(1)} copy-done((bf16[256,1024]{1,0:T(8,128)(2,1)S(1)}, bf16[256,1024]{1,0:T(8,128)(2,1)}, u32[]{:S(2)}) %copy-start.1) | copy-done | bytes 524312
  3.9 0.0 copy-start.2
  3.9 1.0 %copy-done.2 = bf16[1024,256]{1,0:T(8,128)(2,1)S(1)} copy-done((bf16[1024,256]{1,0:T(8,128)(2,1)S(1)}, bf16[1024,256]{1,0:T(8,128)(2,1)}, u32[]{:S(2)}) %copy-start.2) | copy-done | bytes 524312
  5.0 0.0 copy-start.3
  5.0 1.0 %copy-done.3 = bf16[256,768]{1,0:T(8,128)(2,1)S(1)} copy-done((bf16[256,768]{1,0:T(8,128)(2,1)S(1)}, bf16[256,768]{1,0:T(8,128)(2,1)}, u32[]{:S(2)}) %copy-start.3) | copy-done | bytes 393240
  6.0 62.1 %propagate.1 = f32[1,8,256]{2,1,0:T(8,128)S(1)} custom-call(bf16[1,2,64,256]{3,2,1,0:T(8,128)(2,1)S(1)} %copy-done.5, s32[2,64]{1,0:T(2,128)S(1)} %copy-done.7, f32[4,256]{1,0:T(4,128)S(1)} %copy-done.6, bf16[256,768]{1,0:T(8,128)(2,1)S(1)} %copy-done.3, bf16[256,256]{1,0:T(8,128)(2,1)S(1)} %copy-done.4, f32[1,256]{1,0:T(1,128)S(1)} %bitcast.3, ...), custom_call_target="tpu_custom_call" | custom-call | tf_op jit(solution)/shard_map/propagate/pallas_call | solution.py:365
  68.0 0.6 copy.16
Async XLA Ops:
  0.0 2.2 %copy-start = (bf16[256,1024]{1,0:T(8,128)(2,1)S(1)}, bf16[256,1024]{1,0:T(8,128)(2,1)}, u32[]{:S(2)}) copy-start(bf16[256,1024]{1,0:T(8,128)(2,1)} %kp.1) | copy-start | bytes 1572868
  0.8 1.4 %copy-start.4 = (bf16[256,256]{1,0:T(8,128)(2,1)S(1)}, bf16[256,256]{1,0:T(8,128)(2,1)}, u32[]{:S(2)}) copy-start(bf16[256,256]{1,0:T(8,128)(2,1)} %eo.1) | copy-start | bytes 393220
  0.8 1.4 %copy-start.5 = (bf16[1,2,64,256]{3,2,1,0:T(8,128)(2,1)S(1)}, bf16[1,2,64,256]{3,2,1,0:T(8,128)(2,1)}, u32[]{:S(2)}) copy-start(bf16[1,2,64,256]{3,2,1,0:T(8,128)(2,1)} %frames.1) | copy-start | bytes 196612
  0.9 1.4 %copy-start.6 = (f32[4,256]{1,0:T(4,128)S(1)}, f32[4,256]{1,0:T(4,128)}, u32[]{:S(2)}) copy-start(f32[4,256]{1,0:T(4,128)} %table.1) | copy-start | bytes 12292
  0.9 1.4 %copy-start.8 = (f32[256]{0:T(256)S(1)}, f32[256]{0:T(256)}, u32[]{:S(2)}) copy-start(f32[256]{0:T(256)} %param.17) | copy-start | bytes 3076
  2.2 0.7 copy-start.7
  2.2 0.7 copy-start.9
  2.9 1.0 %copy-start.1 = (bf16[256,1024]{1,0:T(8,128)(2,1)S(1)}, bf16[256,1024]{1,0:T(8,128)(2,1)}, u32[]{:S(2)}) copy-start(bf16[256,1024]{1,0:T(8,128)(2,1)} %vp.1) | copy-start | bytes 1572868
  3.9 1.0 %copy-start.2 = (bf16[1024,256]{1,0:T(8,128)(2,1)S(1)}, bf16[1024,256]{1,0:T(8,128)(2,1)}, u32[]{:S(2)}) copy-start(bf16[1024,256]{1,0:T(8,128)(2,1)} %rp.1) | copy-start | bytes 1572868
  5.0 1.0 %copy-start.3 = (bf16[256,768]{1,0:T(8,128)(2,1)S(1)}, bf16[256,768]{1,0:T(8,128)(2,1)}, u32[]{:S(2)}) copy-start(bf16[256,768]{1,0:T(8,128)(2,1)} %qkv.1) | copy-start | bytes 1179652

commit v2 on v1

--- a/solution.py
+++ b/solution.py
@@ -54,7 +54,7 @@
     out,
     x_v, lab_v, tab_v, qkv_v, eo_v, gain_v, kp_v, vp_v, rp_v, dec_v, conv_v, up_v,
     wq_t, eo_t, kp_t, vp_t, tab_t, gain_b, taps_t, up_x, spread,
-    pool, hot, xt, kmask, v_t, e_t, e_tmp, k_t,
+    pool, hot, xt, kmask, v_mask, weights, e_t, e_tmp, k_t,
     state, states, decays, decay_own, memories, memory,
     conved, part, parts,
     load, send, pool_in, hot_in, xt_in, decay_in, state_in, memory_in, part_in,
@@ -170,16 +170,17 @@
     tab_t[...] = turned(jnp.concatenate(three_parts(tab), axis=0))
     gain_b[...] = jnp.broadcast_to(gain_v[...], (TOK, DIM)).T
 
+    here = jnp.where(iota((DIM, HEAD), 0) == sp * HEAD + iota((DIM, HEAD), 1), 1.0, 0.0).astype(BF16)
+
     @pl.loop(0, TAPS)
     def _(n):
-        tap = conv_v[n]
-        both = mm(rp_v[...], tap).T.astype(BF16)
-        own = conv_v[n, pl.ds(pl.multiple_of(sp * HEAD, HEAD), HEAD), :].astype(F32).T.astype(BF16)
+        both = mm_nt(conv_v[n], rp_v[...]).astype(BF16)
+        own = mm(conv_v[n], here).astype(BF16)
         taps_t[pl.ds(pl.multiple_of(n * CH, CH), CH), :] = jnp.concatenate([both, own], axis=1)
 
     row, src_row = iota((32, 16), 0), iota((32, 16), 1)
     picks = jnp.where(src_row == 4 * lax.rem(row, 4) + row // 8, 1.0, 0.0).astype(BF16)
-    up_x[...] = mm_nt(picks, up_v[...]).astype(BF16)
+    up_x[...] = mm(picks, up_v[...]).astype(BF16)
     er, ec = iota((4 * TOK, DIM), 0), iota((4 * TOK, DIM), 1)
     spread[...] = jnp.where(ec == 4 * lax.rem(er, 64) + er // TOK, 1.0, 0.0).astype(BF16)
 
@@ -187,10 +188,11 @@
     pooled = pool[...].reshape(BANDS * TOK // 4, DIM)
     kv = mm(pooled, qkv_v[:, DIM:])
     keys = kv[:, :DIM].astype(BF16)
-    v_t[...] = kv[:, DIM:].T.astype(BF16)
-    lane_head = iota((DIM, DIM), 1) // HEAD
+    values = kv[:, DIM:].T.astype(BF16)
+    lane_head, row_head = iota((DIM, DIM), 1) // HEAD, iota((DIM, DIM), 0) // HEAD
     for h in range(HEADS):
-        kmask[h] = jnp.where(lane_head == h, keys, jnp.zeros_like(keys))
+        kmask[h * DIM : (h + 1) * DIM, :] = jnp.where(lane_head == h, keys, jnp.zeros_like(keys))
+        v_mask[:, h * DIM : (h + 1) * DIM] = jnp.where(row_head == h, values, jnp.zeros_like(values))
     arrived(hot.at[pl.ds(0, BANDS - 1)], hot_in)
 
     state[...] = jnp.zeros_like(state)
@@ -208,14 +210,18 @@
         b0, b1 = lax.rem(sp + BANDS - k0, BANDS), lax.rem(sp + BANDS - k1, BANDS)
         xp = jnp.concatenate([xt[b0], xt[b1]], axis=1)
         q = mm(wq_t[...], xp).astype(BF16)
-        attended = []
+        scores = mm(kmask[...], q)
+        inverse = []
         for h in range(HEADS):
-            s = mm(kmask[h], q)
+            s = scores[h * DIM : (h + 1) * DIM]
             w = jnp.exp2((s - jnp.max(s, axis=0, keepdims=True)) * factor)
-            total = jnp.sum(w, axis=0, keepdims=True)
-            a = mm(v_t[h * HEAD : (h + 1) * HEAD, :], w.astype(BF16))
-            attended.append((a / total).astype(BF16))
-        hidden = xp.astype(F32) + mm(eo_t[...], jnp.concatenate(attended, axis=0))
+            inverse.append(
+                jnp.broadcast_to(1.0 / jnp.sum(w, axis=0, keepdims=True), (HEAD, 2 * TOK))
+            )
+            weights[h * DIM : (h + 1) * DIM, :] = w.astype(BF16)
+        summed = mm(v_mask[...], weights[...])
+        attended = (summed * jnp.concatenate(inverse, axis=0)).astype(BF16)
+        hidden = xp.astype(F32) + mm(eo_t[...], attended)
         scale = lax.rsqrt(jnp.mean(hidden * hidden, axis=0, keepdims=True) + 1e-06)
         gains = jnp.concatenate([gain_b[...], gain_b[...]], axis=1)
         encoded = (hidden * scale * gains).astype(BF16)
@@ -349,12 +355,13 @@
         vmem((2, 64, DIM), BF16), vmem((2, 64), jnp.int32), vmem((4, DIM), F32),
         vmem((DIM, 3 * DIM), BF16), vmem((DIM, DIM), BF16), vmem((1, DIM), F32),
         vmem((DIM, FEAT), BF16), vmem((DIM, FEAT), BF16), vmem((FEAT, DIM), BF16),
-        vmem((1, HEADS), F32), vmem((TAPS, DIM, CH), BF16), vmem((CH, 16), BF16),
+        vmem((1, HEADS), F32), vmem((TAPS, CH, DIM), BF16), vmem((16, CH), BF16),
         vmem((DIM, DIM), BF16), vmem((DIM, DIM), BF16), vmem((FEAT, DIM), BF16),
         vmem((FEAT, DIM), BF16), vmem((DIM, 48), BF16), vmem((DIM, TOK), F32),
         vmem((TAPS * CH, FEAT + HEAD), BF16), vmem((32, CH), BF16), vmem((4 * TOK, DIM), BF16),
         vmem((BANDS, TOK // 4, DIM), BF16), vmem((BANDS, 16, TOK), BF16),
-        vmem((BANDS, DIM, TOK), BF16), vmem((HEADS, DIM, DIM), BF16), vmem((DIM, DIM), BF16),
+        vmem((BANDS, DIM, TOK), BF16), vmem((HEADS * DIM, DIM), BF16),
+        vmem((DIM, HEADS * DIM), BF16), vmem((HEADS * DIM, 2 * TOK), BF16),
         vmem((BANDS, HEAD, TOK), BF16), vmem((DIM, 2 * TOK), BF16), vmem((BANDS, FEAT, TOK), BF16),
         vmem((OWNERS, 8, FEAT), F32), vmem((FRAMES, 8, FEAT), F32), vmem((FRAMES, 8, FEAT), F32),
         vmem((8, FEAT), F32), vmem((FRAMES, 8, FEAT), F32), vmem((OWNERS, 8, FEAT), F32),
@@ -365,16 +372,16 @@
     return pl.pallas_call(
         kernel,
         out_shape=jax.ShapeDtypeStruct((1, 8, DIM), F32),
-        in_specs=[pl.BlockSpec(memory_space=pl.ANY)] * 12,
+        in_specs=[pl.BlockSpec(memory_space=pltpu.HBM)] * 12,
         out_specs=pl.BlockSpec(memory_space=pltpu.VMEM),
         scratch_shapes=scratch,
         compiler_params=pltpu.CompilerParams(
-            collective_id=0, has_side_effects=True, vmem_limit_bytes=48 * 1024 * 1024
+            collective_id=0, has_side_effects=True, vmem_limit_bytes=63 * 1024 * 1024
         ),
         name="propagate",
     )(
         frames, labels, table, qkv, eo, gain.reshape(1, DIM), kp, vp, rp, decay,
-        conv.reshape(TAPS, DIM, CH), up,
+        conv.transpose(0, 1, 3, 2).reshape(TAPS, CH, DIM), up.T,
     )
 
 

time: 69.4 us -> 59 us (0.85)
  local copies, waits for them, and re-layouts: 6.48 us -> 1.3 us
  Pallas kernels: 62.1 us -> 57.1 us
    unnamed x23 -> x1, local copies, waits for them, and re-layouts: 6.48 us -> 1.3 us
    pallas_call x1, Pallas kernels: 62.1 us -> 57.1 us  [shards(): pl.pallas_call(kernel, out_shape=jax.ShapeDtypeStruct((1, 8, DIM), F32),...]
where the time goes in v2:
time: 59 us; the launch traced here: 58.4 us
  Pallas kernels  57.1 us (97%)
  local copies, waits for them, and re-layouts  1.3 us (2%)
    pallas_call x1, Pallas kernels, shards(): pl.pallas_call(kernel, out_shape=jax.ShapeDtypeStruct((1, 8, DIM), F32),...  57.1 us
    unnamed x1, local copies, waits for them, and re-layouts  1.3 us

profile of v2, /device:TPU:6, one launch (start us, length us, event | category | flops | bytes accessed | tf_op | source)
XLA Modules:
  0.0 58.4 jit_solution(8417695750070491033)
XLA Ops:
  0.0 57.1 %propagate.1 = f32[1,8,256]{2,1,0:T(8,128)} custom-call(bf16[1,2,64,256]{3,2,1,0:T(8,128)(2,1)} %frames.1, s32[2,64]{1,0:T(2,128)} %labels.1, f32[4,256]{1,0:T(4,128)} %table.1, bf16[256,768]{1,0:T(8,128)(2,1)} %qkv.1, bf16[256,256]{1,0:T(8,128)(2,1)} %eo.1, f32[1,256]{1,0:T(1,128)} %bitcast.7, bf16[256,1024]{1,0:T(8,128)(2,1)} %kp.1, bf16[256,1024]{1,0:T(8,128)(2,1)} %vp.1, ...), custom_call_target="tpu_custom_call" | custom-call | tf_op jit(solution)/shard_map/propagate/pallas_call | solution.py:372
  57.1 1.3 %copy.14 = f32[1,8,256]{2,1,0:T(8,128)} copy(f32[1,8,256]{2,1,0:T(8,128)} %propagate.1) | data formatting | bytes 16384

commit v3 on v2

--- a/solution.py
+++ b/solution.py
@@ -22,6 +22,7 @@
 FEAT = 128
 CH = 64
 TAPS = 9
+SERVED = 3
 FAR_FIRST = (4, 3, 5, 2, 6, 1, 7)
 
 
@@ -54,13 +55,15 @@
     out,
     x_v, lab_v, tab_v, qkv_v, eo_v, gain_v, kp_v, vp_v, rp_v, dec_v, conv_v, up_v,
     wq_t, eo_t, kp_t, vp_t, tab_t, gain_b, taps_t, up_x, spread,
-    pool, hot, xt, kmask, v_mask, weights, e_t, e_tmp, k_t,
+    pool, hot, xt, kmask, v_mask, weights, e_tmp, state_out, state_part, ke_out, ke,
     state, states, decays, decay_own, memories, memory,
     conved, part, parts,
-    load, send, pool_in, hot_in, xt_in, decay_in, state_in, memory_in, part_in,
+    load, send, pool_in, hot_in, xt_in, part_state_in, ke_in, decay_in, state_in, memory_in, part_in,
 ):
     tm, sp = lax.axis_index("tm"), lax.axis_index("space")
     is_owner = lax.rem(tm, STRIDE) == 0
+    side, pair = lax.rem(sp, 2), sp // 2
+    heads = [sp] + [lax.rem(sp + BANDS + (2 * side - 1) * k, BANDS) for k in range(1, SERVED + 1)]
 
     barrier = pltpu.get_barrier_semaphore()
     for k in range(1, BANDS):
@@ -91,12 +94,14 @@
         (table, tab_v),
         (eo, eo_v),
         (gain, gain_v),
-        (kp.at[:, pl.ds(col, FEAT)], kp_v),
-        (vp.at[:, pl.ds(col, FEAT)], vp_v),
         (rp.at[pl.ds(col, FEAT), :], rp_v),
         (conv, conv_v),
         (up, up_v),
     ]
+    for k, h in enumerate(heads):
+        at = pl.ds(pl.multiple_of(h * FEAT, FEAT), FEAT)
+        loads.append((kp.at[:, at], kp_v.at[k]))
+        loads.append((vp.at[:, at], vp_v.at[k]))
     loads = [pltpu.make_async_copy(s, d, load.at[n]) for n, (s, d) in enumerate(loads)]
     for c in loads:
         c.start()
@@ -110,7 +115,7 @@
     lab = lab_v[...]
     lab_row = jnp.concatenate([lab[0:1], lab[1:2]], axis=1)
     hit = (jnp.broadcast_to(lab_row, (16, TOK)) == iota((16, TOK), 0)) & (tm == 0)
-    hot[sp] = jnp.where(hit, 1.0, 0.0).astype(BF16)
+    hot[side] = jnp.where(hit, 1.0, 0.0).astype(BF16)
     loads[2].wait()
     rate = jnp.sum(
         jnp.where(iota((1, HEADS), 1) == sp, dec_v[...], 0.0), axis=1, keepdims=True
@@ -125,13 +130,13 @@
     def _():
         pl.semaphore_wait(barrier, BANDS - 1 + OWNERS)
 
-    def to_band(k, buf, n, sem):
+    def to_band(place, src, dst, n, sem):
         pltpu.make_async_remote_copy(
-            src_ref=buf.at[sp],
-            dst_ref=buf.at[sp],
+            src_ref=src,
+            dst_ref=dst,
             send_sem=send.at[n],
             recv_sem=sem,
-            device_id=(tm, lax.rem(sp + k, BANDS)),
+            device_id=(tm, place),
             device_id_type=MESH,
         ).start()
 
@@ -139,11 +144,10 @@
         pltpu.make_async_copy(ref, ref, sem).wait()
 
     for k in FAR_FIRST:
-        to_band(k, pool, 0, pool_in)
-    xt[sp] = x.astype(F32).T.astype(BF16)
-    for k in (1, 7, 2, 6, 3, 5, 4):
-        to_band(k, hot, 1, hot_in)
-        to_band(k, xt, 2, xt_in.at[k])
+        to_band(lax.rem(sp + k, BANDS), pool.at[sp], pool.at[sp], 0, pool_in)
+    xt[side] = x.astype(F32).T.astype(BF16)
+    to_band(sp + 1 - 2 * side, xt.at[side], xt.at[side], 2, xt_in)
+    to_band(sp + 1 - 2 * side, hot.at[side], hot.at[side], 1, hot_in)
 
     def to_owners(src, dst, n, sem):
         for c in range(OWNERS):
@@ -164,8 +168,9 @@
         c.wait()
     wq_t[...] = turned(qkv_v[:, :DIM])
     eo_t[...] = turned(eo_v[...])
-    kp_t[...] = turned(kp_v[...])
-    vp_t[...] = turned(vp_v[...])
+    for k in range(SERVED + 1):
+        kp_t[k * FEAT : (k + 1) * FEAT, :] = turned(kp_v[k])
+        vp_t[k * FEAT : (k + 1) * FEAT, :] = turned(vp_v[k])
     tab = jnp.concatenate([tab_v[...], jnp.zeros((12, DIM), F32)], axis=0)
     tab_t[...] = turned(jnp.concatenate(three_parts(tab), axis=0))
     gain_b[...] = jnp.broadcast_to(gain_v[...], (TOK, DIM)).T
@@ -193,52 +198,54 @@
     for h in range(HEADS):
         kmask[h * DIM : (h + 1) * DIM, :] = jnp.where(lane_head == h, keys, jnp.zeros_like(keys))
         v_mask[:, h * DIM : (h + 1) * DIM] = jnp.where(row_head == h, values, jnp.zeros_like(values))
-    arrived(hot.at[pl.ds(0, BANDS - 1)], hot_in)
-
-    state[...] = jnp.zeros_like(state)
+
     factor = HEAD**-0.5 * math.log2(math.e)
-
-    @pl.loop(0, BANDS // 2)
-    def _(p):
-        k0, k1 = p, BANDS - 1 - p
-
-        @pl.when(p > 0)
-        def _():
-            arrived(xt.at[0], xt_in.at[k0])
-
-        arrived(xt.at[0], xt_in.at[k1])
-        b0, b1 = lax.rem(sp + BANDS - k0, BANDS), lax.rem(sp + BANDS - k1, BANDS)
-        xp = jnp.concatenate([xt[b0], xt[b1]], axis=1)
-        q = mm(wq_t[...], xp).astype(BF16)
-        scores = mm(kmask[...], q)
-        inverse = []
-        for h in range(HEADS):
-            s = scores[h * DIM : (h + 1) * DIM]
-            w = jnp.exp2((s - jnp.max(s, axis=0, keepdims=True)) * factor)
-            inverse.append(
-                jnp.broadcast_to(1.0 / jnp.sum(w, axis=0, keepdims=True), (HEAD, 2 * TOK))
-            )
-            weights[h * DIM : (h + 1) * DIM, :] = w.astype(BF16)
-        summed = mm(v_mask[...], weights[...])
-        attended = (summed * jnp.concatenate(inverse, axis=0)).astype(BF16)
-        hidden = xp.astype(F32) + mm(eo_t[...], attended)
-        scale = lax.rsqrt(jnp.mean(hidden * hidden, axis=0, keepdims=True) + 1e-06)
-        gains = jnp.concatenate([gain_b[...], gain_b[...]], axis=1)
-        encoded = (hidden * scale * gains).astype(BF16)
-        e_tmp[...] = encoded
-        own = e_tmp[pl.ds(pl.multiple_of(sp * HEAD, HEAD), HEAD), :]
-        e_t[b0] = own[:, :TOK]
-        e_t[b1] = own[:, TOK:]
-        key = mm(kp_t[...], encoded).astype(BF16)
-        k_t[b0] = key[:, :TOK]
-        k_t[b1] = key[:, TOK:]
-        mark = jnp.concatenate([hot[b0], hot[b1]], axis=1)
-        mark = jnp.concatenate([mark, mark, mark], axis=0)
-        told = (encoded.astype(F32) + mm(tab_t[...], mark)).astype(BF16)
-        value = mm(vp_t[...], told).astype(BF16)
-        state[...] += mm_nt(value, key).reshape(OWNERS, 8, FEAT)
-
-    state[...] = state[...] * (BANDS * TOK) ** -0.5
+    arrived(xt.at[0], xt_in)
+    arrived(hot.at[0], hot_in)
+    xp = jnp.concatenate([xt[0], xt[1]], axis=1)
+    q = mm(wq_t[...], xp).astype(BF16)
+    scores = mm(kmask[...], q)
+    inverse = []
+    for h in range(HEADS):
+        s = scores[h * DIM : (h + 1) * DIM]
+        w = jnp.exp2((s - jnp.max(s, axis=0, keepdims=True)) * factor)
+        inverse.append(
+            jnp.broadcast_to(1.0 / jnp.sum(w, axis=0, keepdims=True), (HEAD, 2 * TOK))
+        )
+        weights[h * DIM : (h + 1) * DIM, :] = w.astype(BF16)
+    summed = mm(v_mask[...], weights[...])
+    attended = (summed * jnp.concatenate(inverse, axis=0)).astype(BF16)
+    hidden = xp.astype(F32) + mm(eo_t[...], attended)
+    scale = lax.rsqrt(jnp.mean(hidden * hidden, axis=0, keepdims=True) + 1e-06)
+    gains = jnp.concatenate([gain_b[...], gain_b[...]], axis=1)
+    encoded = (hidden * scale * gains).astype(BF16)
+    e_tmp[...] = encoded
+    mark = jnp.concatenate([hot[0], hot[1]], axis=1)
+    mark = jnp.concatenate([mark, mark, mark], axis=0)
+    told = (encoded.astype(F32) + mm(tab_t[...], mark)).astype(BF16)
+    keys = mm(kp_t[...], encoded).astype(BF16)
+    values = mm(vp_t[...], told).astype(BF16)
+
+    def share(k):
+        at = slice(k * FEAT, (k + 1) * FEAT)
+        return mm_nt(values[at], keys[at]) * (BANDS * TOK) ** -0.5
+
+    for k in range(SERVED, 0, -1):
+        state_out[k - 1] = share(k).astype(BF16)
+        to_band(heads[k], state_out.at[k - 1], state_part.at[k - 1], 7, part_state_in)
+    total = share(0)
+    for k in range(SERVED + 1):
+        h = pl.multiple_of(heads[k] * HEAD, HEAD)
+        both = jnp.concatenate([keys[k * FEAT : (k + 1) * FEAT], e_tmp[pl.ds(h, HEAD), :]], axis=0)
+        if k == 0:
+            ke[pair] = both
+        else:
+            ke_out[k - 1] = both
+            to_band(heads[k], ke_out.at[k - 1], ke.at[pair], 8, ke_in)
+    arrived(state_part, part_state_in)
+    for k in range(SERVED):
+        total = total + state_part[k].astype(F32)
+    state[...] = total.reshape(OWNERS, 8, FEAT)
 
     to_owners(lambda c: state.at[c], states, 4, state_in)
 
@@ -276,11 +283,10 @@
         arrived(memory, memory_in)
 
     now = memory[...].reshape(FEAT, FEAT).astype(BF16)
+    arrived(ke_out, ke_in)
     for p in range(BANDS // 2):
-        key = jnp.concatenate([k_t[2 * p], k_t[2 * p + 1]], axis=1)
-        own = jnp.concatenate([e_t[2 * p], e_t[2 * p + 1]], axis=1)
-        read = (mm(now, key) * FEAT**-0.5).astype(BF16)
-        c = mm(taps_t[...], jnp.concatenate([read, own], axis=0))
+        read = (mm(now, ke[p, :FEAT, :]) * FEAT**-0.5).astype(BF16)
+        c = mm(taps_t[...], jnp.concatenate([read, ke[p, FEAT:, :]], axis=0))
         conved[2 * p] = c[:, :TOK]
         conved[2 * p + 1] = c[:, TOK:]
     lane = iota((CH, TOK), 1)
@@ -331,8 +337,10 @@
     out[0] = high + (mm(middle, spread[...]) + mm(low, spread[...]))
 
     arrived(pool.at[pl.ds(0, BANDS - 1)], send.at[0])
-    arrived(hot.at[pl.ds(0, BANDS - 1)], send.at[1])
-    arrived(xt.at[pl.ds(0, BANDS - 1)], send.at[2])
+    arrived(hot.at[0], send.at[1])
+    arrived(xt.at[0], send.at[2])
+    arrived(state_out, send.at[7])
+    arrived(ke_out, send.at[8])
 
     @pl.when(is_owner)
     def _():
@@ -354,20 +362,21 @@
     scratch = [
         vmem((2, 64, DIM), BF16), vmem((2, 64), jnp.int32), vmem((4, DIM), F32),
         vmem((DIM, 3 * DIM), BF16), vmem((DIM, DIM), BF16), vmem((1, DIM), F32),
-        vmem((DIM, FEAT), BF16), vmem((DIM, FEAT), BF16), vmem((FEAT, DIM), BF16),
+        vmem((SERVED + 1, DIM, FEAT), BF16), vmem((SERVED + 1, DIM, FEAT), BF16), vmem((FEAT, DIM), BF16),
         vmem((1, HEADS), F32), vmem((TAPS, CH, DIM), BF16), vmem((16, CH), BF16),
-        vmem((DIM, DIM), BF16), vmem((DIM, DIM), BF16), vmem((FEAT, DIM), BF16),
-        vmem((FEAT, DIM), BF16), vmem((DIM, 48), BF16), vmem((DIM, TOK), F32),
+        vmem((DIM, DIM), BF16), vmem((DIM, DIM), BF16), vmem(((SERVED + 1) * FEAT, DIM), BF16),
+        vmem(((SERVED + 1) * FEAT, DIM), BF16), vmem((DIM, 48), BF16), vmem((DIM, TOK), F32),
         vmem((TAPS * CH, FEAT + HEAD), BF16), vmem((32, CH), BF16), vmem((4 * TOK, DIM), BF16),
-        vmem((BANDS, TOK // 4, DIM), BF16), vmem((BANDS, 16, TOK), BF16),
-        vmem((BANDS, DIM, TOK), BF16), vmem((HEADS * DIM, DIM), BF16),
+        vmem((BANDS, TOK // 4, DIM), BF16), vmem((2, 16, TOK), BF16),
+        vmem((2, DIM, TOK), BF16), vmem((HEADS * DIM, DIM), BF16),
         vmem((DIM, HEADS * DIM), BF16), vmem((HEADS * DIM, 2 * TOK), BF16),
-        vmem((BANDS, HEAD, TOK), BF16), vmem((DIM, 2 * TOK), BF16), vmem((BANDS, FEAT, TOK), BF16),
+        vmem((DIM, 2 * TOK), BF16), vmem((SERVED, FEAT, FEAT), BF16), vmem((SERVED, FEAT, FEAT), BF16),
+        vmem((SERVED, FEAT + HEAD, 2 * TOK), BF16), vmem((BANDS // 2, FEAT + HEAD, 2 * TOK), BF16),
         vmem((OWNERS, 8, FEAT), F32), vmem((FRAMES, 8, FEAT), F32), vmem((FRAMES, 8, FEAT), F32),
         vmem((8, FEAT), F32), vmem((FRAMES, 8, FEAT), F32), vmem((OWNERS, 8, FEAT), F32),
         vmem((BANDS, TAPS * CH, TOK), F32), vmem((BANDS, CH, TOK), BF16),
         vmem((BANDS, CH, TOK), BF16),
-        dma((12,)), dma((7,)), dma, dma, dma((BANDS,)), dma, dma, dma, dma,
+        dma((18,)), dma((9,)), dma, dma, dma, dma, dma, dma, dma, dma, dma,
     ]
     return pl.pallas_call(
         kernel,

time: 59 us -> 50.6 us (0.86)
  Pallas kernels: 57.1 us -> 48.5 us
    pallas_call x1, Pallas kernels: 57.1 us -> 48.5 us  [shards(): pl.pallas_call(kernel, out_shape=jax.ShapeDtypeStruct((1, 8, DIM), F32),...]
where the time goes in v3:
time: 50.6 us; the launch traced here: 49.8 us
  Pallas kernels  48.5 us (96%)
  local copies, waits for them, and re-layouts  1.3 us (3%)
    pallas_call x1, Pallas kernels, shards(): pl.pallas_call(kernel, out_shape=jax.ShapeDtypeStruct((1, 8, DIM), F32),...  48.5 us
    unnamed x1, local copies, waits for them, and re-layouts  1.3 us

profile of v3, /device:TPU:6, one launch (start us, length us, event | category | flops | bytes accessed | tf_op | source)
XLA Modules:
  0.0 49.8 jit_solution(2503226592541578152)
XLA Ops:
  0.0 48.5 %propagate.1 = f32[1,8,256]{2,1,0:T(8,128)} custom-call(bf16[1,2,64,256]{3,2,1,0:T(8,128)(2,1)} %frames.1, s32[2,64]{1,0:T(2,128)} %labels.1, f32[4,256]{1,0:T(4,128)} %table.1, bf16[256,768]{1,0:T(8,128)(2,1)} %qkv.1, bf16[256,256]{1,0:T(8,128)(2,1)} %eo.1, f32[1,256]{1,0:T(1,128)} %bitcast.7, bf16[256,1024]{1,0:T(8,128)(2,1)} %kp.1, bf16[256,1024]{1,0:T(8,128)(2,1)} %vp.1, ...), custom_call_target="tpu_custom_call" | custom-call | tf_op jit(solution)/shard_map/propagate/pallas_call | solution.py:381
  48.5 1.3 %copy.14 = f32[1,8,256]{2,1,0:T(8,128)} copy(f32[1,8,256]{2,1,0:T(8,128)} %propagate.1) | data formatting | bytes 16384

commit v4 on v3

--- a/solution.py
+++ b/solution.py
@@ -58,32 +58,35 @@
     pool, hot, xt, kmask, v_mask, weights, e_tmp, state_out, state_part, ke_out, ke,
     state, states, decays, decay_own, memories, memory,
     conved, part, parts,
-    load, send, pool_in, hot_in, xt_in, part_state_in, ke_in, decay_in, state_in, memory_in, part_in,
+    load, send, greetings, pool_in, hot_in, xt_in, part_state_in, ke_in, decay_in, state_in, memory_in, part_in,
 ):
     tm, sp = lax.axis_index("tm"), lax.axis_index("space")
     is_owner = lax.rem(tm, STRIDE) == 0
     side, pair = lax.rem(sp, 2), sp // 2
     heads = [sp] + [lax.rem(sp + BANDS + (2 * side - 1) * k, BANDS) for k in range(1, SERVED + 1)]
 
+    core, y, x = lax.rem(tm, 2), lax.rem(tm // 2, 8), tm // 16
+    along_y = [x * 16 + lax.rem(y + k, 8) * 2 + core for k in (1, 7)]
+    along_x = [lax.rem(x + k, 4) * 16 + y * 2 + core for k in (1, 3)]
+
     barrier = pltpu.get_barrier_semaphore()
     for k in range(1, BANDS):
         pl.semaphore_signal(
             barrier, inc=1, device_id=(tm, lax.rem(sp + k, BANDS)), device_id_type=MESH
         )
 
-    @pl.when(is_owner)
-    def _():
-        @pl.loop(1, FRAMES)
-        def _(k):
+    partner = 1 - 2 * core
+    for t in (*along_y, *along_x, *(t + partner for t in along_y), tm + partner):
+        pl.semaphore_signal(barrier, inc=1, device_id=(t, sp), device_id_type=MESH)
+
+    def greet(n):
+        for t in along_y if n < 3 else along_x:
             pl.semaphore_signal(
-                barrier, inc=1, device_id=(lax.rem(tm + k, FRAMES), sp), device_id_type=MESH
+                greetings.at[n], inc=1, device_id=(t, sp), device_id_type=MESH
             )
 
-    @pl.when(jnp.logical_not(is_owner))
-    def _():
-        @pl.loop(0, OWNERS)
-        def _(k):
-            pl.semaphore_signal(barrier, inc=1, device_id=(k * STRIDE, sp), device_id_type=MESH)
+    def greeted(n):
+        pl.semaphore_wait(greetings.at[n], 2)
 
     col = pl.multiple_of(sp * FEAT, FEAT)
     loads = [
@@ -107,10 +110,10 @@
         c.start()
 
     loads[0].wait()
-    x = x_v[...].reshape(TOK, DIM)
+    own = x_v[...].reshape(TOK, DIM)
     pr, pc = iota((TOK // 4, TOK), 0), iota((TOK // 4, TOK), 1)
     quarter = jnp.where(lax.rem(pc, 64) // 2 == pr, 0.25, 0.0).astype(BF16)
-    pool[sp] = mm(quarter, x).astype(BF16)
+    pool[sp] = mm(quarter, own).astype(BF16)
     loads[1].wait()
     lab = lab_v[...]
     lab_row = jnp.concatenate([lab[0:1], lab[1:2]], axis=1)
@@ -122,13 +125,7 @@
     )
     decay_own[...] = jnp.broadcast_to(rate, (8, FEAT))
 
-    @pl.when(is_owner)
-    def _():
-        pl.semaphore_wait(barrier, BANDS - 1 + FRAMES - 1)
-
-    @pl.when(jnp.logical_not(is_owner))
-    def _():
-        pl.semaphore_wait(barrier, BANDS - 1 + OWNERS)
+    pl.semaphore_wait(barrier, BANDS - 1 + 7)
 
     def to_band(place, src, dst, n, sem):
         pltpu.make_async_remote_copy(
@@ -145,7 +142,7 @@
 
     for k in FAR_FIRST:
         to_band(lax.rem(sp + k, BANDS), pool.at[sp], pool.at[sp], 0, pool_in)
-    xt[side] = x.astype(F32).T.astype(BF16)
+    xt[side] = own.astype(F32).T.astype(BF16)
     to_band(sp + 1 - 2 * side, xt.at[side], xt.at[side], 2, xt_in)
     to_band(sp + 1 - 2 * side, hot.at[side], hot.at[side], 1, hot_in)
 
@@ -162,32 +159,21 @@
                     device_id_type=MESH,
                 ).start()
 
-    to_owners(lambda c: decay_own, decays, 3, decay_in)
-
+    greet(0)
     for c in loads[3:]:
         c.wait()
     wq_t[...] = turned(qkv_v[:, :DIM])
     eo_t[...] = turned(eo_v[...])
+    greeted(0)
+    greet(1)
     for k in range(SERVED + 1):
         kp_t[k * FEAT : (k + 1) * FEAT, :] = turned(kp_v[k])
         vp_t[k * FEAT : (k + 1) * FEAT, :] = turned(vp_v[k])
+    greeted(1)
+    greet(2)
     tab = jnp.concatenate([tab_v[...], jnp.zeros((12, DIM), F32)], axis=0)
     tab_t[...] = turned(jnp.concatenate(three_parts(tab), axis=0))
     gain_b[...] = jnp.broadcast_to(gain_v[...], (TOK, DIM)).T
-
-    here = jnp.where(iota((DIM, HEAD), 0) == sp * HEAD + iota((DIM, HEAD), 1), 1.0, 0.0).astype(BF16)
-
-    @pl.loop(0, TAPS)
-    def _(n):
-        both = mm_nt(conv_v[n], rp_v[...]).astype(BF16)
-        own = mm(conv_v[n], here).astype(BF16)
-        taps_t[pl.ds(pl.multiple_of(n * CH, CH), CH), :] = jnp.concatenate([both, own], axis=1)
-
-    row, src_row = iota((32, 16), 0), iota((32, 16), 1)
-    picks = jnp.where(src_row == 4 * lax.rem(row, 4) + row // 8, 1.0, 0.0).astype(BF16)
-    up_x[...] = mm(picks, up_v[...]).astype(BF16)
-    er, ec = iota((4 * TOK, DIM), 0), iota((4 * TOK, DIM), 1)
-    spread[...] = jnp.where(ec == 4 * lax.rem(er, 64) + er // TOK, 1.0, 0.0).astype(BF16)
 
     arrived(pool.at[pl.ds(0, BANDS - 1)], pool_in)
     pooled = pool[...].reshape(BANDS * TOK // 4, DIM)
@@ -198,6 +184,9 @@
     for h in range(HEADS):
         kmask[h * DIM : (h + 1) * DIM, :] = jnp.where(lane_head == h, keys, jnp.zeros_like(keys))
         v_mask[:, h * DIM : (h + 1) * DIM] = jnp.where(row_head == h, values, jnp.zeros_like(values))
+
+    greeted(2)
+    greet(3)
 
     factor = HEAD**-0.5 * math.log2(math.e)
     arrived(xt.at[0], xt_in)
@@ -215,6 +204,8 @@
         weights[h * DIM : (h + 1) * DIM, :] = w.astype(BF16)
     summed = mm(v_mask[...], weights[...])
     attended = (summed * jnp.concatenate(inverse, axis=0)).astype(BF16)
+    greeted(3)
+    greet(4)
     hidden = xp.astype(F32) + mm(eo_t[...], attended)
     scale = lax.rsqrt(jnp.mean(hidden * hidden, axis=0, keepdims=True) + 1e-06)
     gains = jnp.concatenate([gain_b[...], gain_b[...]], axis=1)
@@ -242,6 +233,23 @@
         else:
             ke_out[k - 1] = both
             to_band(heads[k], ke_out.at[k - 1], ke.at[pair], 8, ke_in)
+    greeted(4)
+    to_owners(lambda c: decay_own, decays, 3, decay_in)
+
+    here = jnp.where(iota((DIM, HEAD), 0) == sp * HEAD + iota((DIM, HEAD), 1), 1.0, 0.0).astype(BF16)
+
+    @pl.loop(0, TAPS)
+    def _(n):
+        both = mm_nt(conv_v[n], rp_v[...]).astype(BF16)
+        own = mm(conv_v[n], here).astype(BF16)
+        taps_t[pl.ds(pl.multiple_of(n * CH, CH), CH), :] = jnp.concatenate([both, own], axis=1)
+
+    row, src_row = iota((32, 16), 0), iota((32, 16), 1)
+    picks = jnp.where(src_row == 4 * lax.rem(row, 4) + row // 8, 1.0, 0.0).astype(BF16)
+    up_x[...] = mm(picks, up_v[...]).astype(BF16)
+    er, ec = iota((4 * TOK, DIM), 0), iota((4 * TOK, DIM), 1)
+    spread[...] = jnp.where(ec == 4 * lax.rem(er, 64) + er // TOK, 1.0, 0.0).astype(BF16)
+
     arrived(state_part, part_state_in)
     for k in range(SERVED):
         total = total + state_part[k].astype(F32)
@@ -376,7 +384,7 @@
         vmem((8, FEAT), F32), vmem((FRAMES, 8, FEAT), F32), vmem((OWNERS, 8, FEAT), F32),
         vmem((BANDS, TAPS * CH, TOK), F32), vmem((BANDS, CH, TOK), BF16),
         vmem((BANDS, CH, TOK), BF16),
-        dma((18,)), dma((9,)), dma, dma, dma, dma, dma, dma, dma, dma, dma,
+        dma((18,)), dma((9,)), pltpu.SemaphoreType.REGULAR((5,)), dma, dma, dma, dma, dma, dma, dma, dma, dma,
     ]
     return pl.pallas_call(
         kernel,

time: 50.6 us -> 47.8 us (0.945)
  Pallas kernels: 48.5 us -> 45.8 us
    pallas_call x1, Pallas kernels: 48.5 us -> 45.8 us  [shards(): pl.pallas_call(kernel, out_shape=jax.ShapeDtypeStruct((1, 8, DIM), F32),...]
where the time goes in v4:
time: 47.8 us; the launch traced here: 47.1 us
  Pallas kernels  45.8 us (96%)
  local copies, waits for them, and re-layouts  1.3 us (3%)
    pallas_call x1, Pallas kernels, shards(): pl.pallas_call(kernel, out_shape=jax.ShapeDtypeStruct((1, 8, DIM), F32),...  45.8 us
    unnamed x1, local copies, waits for them, and re-layouts  1.3 us

profile of v4, /device:TPU:6, one launch (start us, length us, event | category | flops | bytes accessed | tf_op | source)
XLA Modules:
  0.0 47.1 jit_solution(16487520779375460065)
XLA Ops:
  0.0 45.8 %propagate.1 = f32[1,8,256]{2,1,0:T(8,128)} custom-call(bf16[1,2,64,256]{3,2,1,0:T(8,128)(2,1)} %frames.1, s32[2,64]{1,0:T(2,128)} %labels.1, f32[4,256]{1,0:T(4,128)} %table.1, bf16[256,768]{1,0:T(8,128)(2,1)} %qkv.1, bf16[256,256]{1,0:T(8,128)(2,1)} %eo.1, f32[1,256]{1,0:T(1,128)} %bitcast.7, bf16[256,1024]{1,0:T(8,128)(2,1)} %kp.1, bf16[256,1024]{1,0:T(8,128)(2,1)} %vp.1, ...), custom_call_target="tpu_custom_call" | custom-call | tf_op jit(solution)/shard_map/propagate/pallas_call | solution.py:389
  45.8 1.3 %copy.14 = f32[1,8,256]{2,1,0:T(8,128)} copy(f32[1,8,256]{2,1,0:T(8,128)} %propagate.1) | data formatting | bytes 16384

commit v5 on v4

--- a/solution.py
+++ b/solution.py
@@ -140,6 +140,7 @@
     def arrived(ref, sem):
         pltpu.make_async_copy(ref, ref, sem).wait()
 
+    greet(0)
     for k in FAR_FIRST:
         to_band(lax.rem(sp + k, BANDS), pool.at[sp], pool.at[sp], 0, pool_in)
     xt[side] = own.astype(F32).T.astype(BF16)
@@ -159,7 +160,6 @@
                     device_id_type=MESH,
                 ).start()
 
-    greet(0)
     for c in loads[3:]:
         c.wait()
     wq_t[...] = turned(qkv_v[:, :DIM])

time: 47.8 us -> 47.7 us (level)
  no operation moved by 1% of the time
where the time goes in v5:
time: 47.7 us; the launch traced here: 47 us
  Pallas kernels  45.7 us (96%)
  local copies, waits for them, and re-layouts  1.3 us (3%)
    pallas_call x1, Pallas kernels, shards(): pl.pallas_call(kernel, out_shape=jax.ShapeDtypeStruct((1, 8, DIM), F32),...  45.7 us
    unnamed x1, local copies, waits for them, and re-layouts  1.3 us

profile of v5, /device:TPU:6, one launch (start us, length us, event | category | flops | bytes accessed | tf_op | source)
XLA Modules:
  0.0 47.0 jit_solution(3699783661041139976)
XLA Ops:
  0.0 45.7 %propagate.1 = f32[1,8,256]{2,1,0:T(8,128)} custom-call(bf16[1,2,64,256]{3,2,1,0:T(8,128)(2,1)} %frames.1, s32[2,64]{1,0:T(2,128)} %labels.1, f32[4,256]{1,0:T(4,128)} %table.1, bf16[256,768]{1,0:T(8,128)(2,1)} %qkv.1, bf16[256,256]{1,0:T(8,128)(2,1)} %eo.1, f32[1,256]{1,0:T(1,128)} %bitcast.7, bf16[256,1024]{1,0:T(8,128)(2,1)} %kp.1, bf16[256,1024]{1,0:T(8,128)(2,1)} %vp.1, ...), custom_call_target="tpu_custom_call" | custom-call | tf_op jit(solution)/shard_map/propagate/pallas_call | solution.py:389
  45.7 1.3 %copy.14 = f32[1,8,256]{2,1,0:T(8,128)} copy(f32[1,8,256]{2,1,0:T(8,128)} %propagate.1) | data formatting | bytes 16384

commit v6 on v5

--- a/solution.py
+++ b/solution.py
@@ -255,14 +255,13 @@
         total = total + state_part[k].astype(F32)
     state[...] = total.reshape(OWNERS, 8, FEAT)
 
-    to_owners(lambda c: state.at[c], states, 4, state_in)
+    to_owners(lambda c: state.at[c], states, 4, state_in.at[x])
 
     @pl.when(is_owner)
     def _():
         states[tm] = state[tm // STRIDE]
         decays[tm] = decay_own[...]
         arrived(decays.at[pl.ds(0, FRAMES - 1)], decay_in)
-        arrived(states.at[pl.ds(0, FRAMES - 1)], state_in)
         place = tm // STRIDE
 
         def frame(t, held):
@@ -282,7 +281,17 @@
 
             return held + states[t]
 
-        lax.fori_loop(0, FRAMES, frame, jnp.zeros((8, FEAT), F32))
+        held = jnp.zeros((8, FEAT), F32)
+        for g in range(4):
+            @pl.when(x == g)
+            def _():
+                arrived(states.at[pl.ds(0, FRAMES // 4 - 1)], state_in.at[g])
+
+            @pl.when(x != g)
+            def _():
+                arrived(states.at[pl.ds(0, FRAMES // 4)], state_in.at[g])
+
+            held = lax.fori_loop(g * FRAMES // 4, (g + 1) * FRAMES // 4, frame, held)
         memory[place] = memories[tm]
         arrived(memory.at[pl.ds(0, OWNERS - 1)], memory_in)
 
@@ -384,7 +393,7 @@
         vmem((8, FEAT), F32), vmem((FRAMES, 8, FEAT), F32), vmem((OWNERS, 8, FEAT), F32),
         vmem((BANDS, TAPS * CH, TOK), F32), vmem((BANDS, CH, TOK), BF16),
         vmem((BANDS, CH, TOK), BF16),
-        dma((18,)), dma((9,)), pltpu.SemaphoreType.REGULAR((5,)), dma, dma, dma, dma, dma, dma, dma, dma, dma,
+        dma((18,)), dma((9,)), pltpu.SemaphoreType.REGULAR((5,)), dma, dma, dma, dma, dma, dma, dma((4,)), dma, dma,
     ]
     return pl.pallas_call(
         kernel,

time: 47.7 us -> 47.7 us (level)
  no operation moved by 1% of the time
where the time goes in v6:
time: 47.7 us; the launch traced here: 47 us
  Pallas kernels  45.7 us (96%)
  local copies, waits for them, and re-layouts  1.3 us (3%)
    pallas_call x1, Pallas kernels, shards(): pl.pallas_call(kernel, out_shape=jax.ShapeDtypeStruct((1, 8, DIM), F32),...  45.7 us
    unnamed x1, local copies, waits for them, and re-layouts  1.3 us

profile of v6, /device:TPU:6, one launch (start us, length us, event | category | flops | bytes accessed | tf_op | source)
XLA Modules:
  0.0 47.0 jit_solution(3642244571176675438)
XLA Ops:
  0.0 45.7 %propagate.1 = f32[1,8,256]{2,1,0:T(8,128)} custom-call(bf16[1,2,64,256]{3,2,1,0:T(8,128)(2,1)} %frames.1, s32[2,64]{1,0:T(2,128)} %labels.1, f32[4,256]{1,0:T(4,128)} %table.1, bf16[256,768]{1,0:T(8,128)(2,1)} %qkv.1, bf16[256,256]{1,0:T(8,128)(2,1)} %eo.1, f32[1,256]{1,0:T(1,128)} %bitcast.7, bf16[256,1024]{1,0:T(8,128)(2,1)} %kp.1, bf16[256,1024]{1,0:T(8,128)(2,1)} %vp.1, ...), custom_call_target="tpu_custom_call" | custom-call | tf_op jit(solution)/shard_map/propagate/pallas_call | solution.py:398
  45.7 1.3 %copy.14 = f32[1,8,256]{2,1,0:T(8,128)} copy(f32[1,8,256]{2,1,0:T(8,128)} %propagate.1) | data formatting | bytes 16384
